TPU v7x, 32 devices: a whole 2x2x4 slice. The times are simulated.
32 devices in a mesh: freq: 8 (over y, x, core), blk: 4 (over z).
Axes of the slice: x: 2, y: 2, z: 4, core: 2. Of those that a mesh axis runs over, the one named last changes fastest.
Arguments:
- traces: bfloat16 [32, 4096, 1024], P(('blk', 'freq')), may hold values from -6 to 6
- fir: float32 [128], replicated, may hold values from -0.5 to 0.5
- targets: int32 [256], replicated, may hold values from 0 to 31
- band: int32 [2], replicated, may hold values from 1 to 512, as said below
Outputs:
- multiples: float32 [32, 2, 256, 4096], P('freq', None, None, 'blk')
Inputs may be any that keep to these rules, and one draw needn't show every extreme that they name: band[1] is 512 and band[1] - band[0] is at least 256.
All inputs are finite; a program needn't handle non-finite values.
Results may differ from a plain program's by a relative error of at most 0.019.
Values may be sent and summed in bfloat16 or wider, within the bound.
A program may use at most 128 MiB of HBM per device.

v0:
```python
import math
import jax
import jax.numpy as jnp
from jax import lax
from jax.sharding import PartitionSpec as P

FREQ_DEV = 4


def phase_table(band, freq_count, time_count):
    band_low = band[0]
    band_high = band[1]
    freq_index = jnp.arange(freq_count, dtype=jnp.int32)
    numerator = band_low * freq_count + (band_high - band_low) * freq_index
    time_index = jnp.arange(time_count, dtype=jnp.int32)
    turn_count = jnp.mod(time_index[:, None] * numerator[None, :], freq_count * time_count)
    phase_angle = turn_count.astype(jnp.float32) * (2.0 * math.pi / (freq_count * time_count))
    table = jnp.stack([jnp.cos(phase_angle), -jnp.sin(phase_angle)], axis=2) * (
        1.0 / math.sqrt(time_count)
    )
    return table.reshape(time_count, 2 * freq_count)


def split_parts(values):
    high_part = values.astype(jnp.bfloat16)
    low_part = (values - high_part.astype(jnp.float32)).astype(jnp.bfloat16)
    return (high_part, low_part)


def block_left(chosen):
    return jnp.stack(
        [
            jnp.concatenate([chosen[:, 0], -chosen[:, 1]], 1),
            jnp.concatenate([chosen[:, 1], chosen[:, 0]], 1),
        ],
        1,
    )


def column_products(chosen, columns, weight_scale):
    freq_dev, parts, shot_count, col_width = columns.shape
    right_block = columns.reshape(freq_dev, 2 * shot_count, col_width)
    summed = jnp.einsum(
        "fojk,fjr->fokr", block_left(chosen), right_block, preferred_element_type=jnp.float32
    )
    return summed * weight_scale


def local_targets(columns, targets, col_stride):
    picked = jnp.take(columns[..., ::col_stride], targets, axis=2)
    return jnp.swapaxes(picked, 2, 3)


def section_plan(spectrum, targets, col_stride, weight_scale):
    row_layout = lax.all_to_all(spectrum, "freq", split_axis=0, concat_axis=2, tiled=True)
    columns = lax.all_to_all(row_layout, "blk", split_axis=3, concat_axis=2, tiled=True)
    chosen = lax.all_gather(local_targets(columns, targets, col_stride), "blk", axis=2, tiled=True)
    return column_products(chosen, columns, weight_scale)


def per_device(traces, fir, targets, band):
    shot_dev, rec_count, time_count = traces.shape
    freq_devs = lax.axis_size("freq")
    blk_devs = lax.axis_size("blk")
    freq_count = FREQ_DEV * freq_devs
    shot_count = shot_dev * freq_devs * blk_devs
    col_stride = rec_count // shot_count
    tap_count = fir.shape[0]
    block_count = time_count // tap_count
    row_total = shot_dev * rec_count
    dft_table = phase_table(band, freq_count, time_count).reshape(
        block_count, tap_count, 2 * freq_count
    )
    tap_index = jnp.arange(tap_count, dtype=jnp.int32)
    lag_table = jnp.mod(tap_index[None, :] - tap_index[:, None], tap_count)
    circulant = jnp.sum(
        jnp.where(lag_table[:, :, None] == tap_index[None, None, :], fir[None, None, :], 0.0),
        axis=2,
    )
    lower_part = jnp.where(tap_index[None, :] >= tap_index[:, None], circulant, 0.0)
    upper_part = jnp.where(tap_index[None, :] < tap_index[:, None], circulant, 0.0)
    signal = traces.reshape(row_total, block_count, tap_count)
    lower_high, lower_low = split_parts(lower_part)
    upper_high, upper_low = split_parts(upper_part)
    earlier = signal[:, :-1]
    carried = jnp.einsum("rna,ab->rnb", earlier, upper_high, preferred_element_type=jnp.float32)
    carried = carried + jnp.einsum(
        "rna,ab->rnb", earlier, upper_low, preferred_element_type=jnp.float32
    )
    carried = jnp.concatenate([jnp.zeros((row_total, 1, tap_count), jnp.float32), carried], 1)
    shaped = jnp.einsum("rna,ab->rnb", signal, lower_high, preferred_element_type=jnp.float32)
    shaped = (
        shaped
        + jnp.einsum("rna,ab->rnb", signal, lower_low, preferred_element_type=jnp.float32)
        + carried
    )
    shaped_high, shaped_low = split_parts(shaped)
    table_high, table_low = split_parts(dft_table)
    spectrum = jnp.einsum(
        "rnb,nbc->cr", shaped_high, table_high, preferred_element_type=jnp.float32
    )
    spectrum = spectrum + jnp.einsum(
        "rnb,nbc->cr", shaped_high, table_low, preferred_element_type=jnp.float32
    )
    spectrum = spectrum + jnp.einsum(
        "rnb,nbc->cr", shaped_low, table_high, preferred_element_type=jnp.float32
    )
    spectrum = spectrum.astype(jnp.bfloat16).reshape(freq_count, 2, shot_dev, rec_count)
    weight_scale = 1.0 / math.sqrt(shot_count)
    return section_plan(spectrum, targets, col_stride, weight_scale)


def solution(mesh):
    placed = (P(("blk", "freq"), None, None), P(), P(), P())
    return jax.shard_map(
        per_device,
        mesh=mesh,
        in_specs=placed,
        out_specs=P("freq", None, None, "blk"),
        check_vma=False,
    )
```

profile of v0, /device:TPU:0, one launch (start us, length us, event | category | flops | bytes accessed | tf_op | source)
XLA Modules:
  0.0 191.2 jit_solution(4319317506778272300)
XLA Ops:
  0.0 0.0 copy-start.4
  0.0 11.9 %copy.90 = bf16[1,4096,1024]{1,2,0:T(8,128)(2,1)} copy(bf16[1,4096,1024]{2,1,0:T(8,128)(2,1)} %param.4) | data formatting | bytes 16777216 | tf_op args[0]
  12.0 0.0 copy-done.4
  12.0 5.1 %select_reduce_fusion = f32[128,128]{1,0:T(8,128)S(1)} fusion(f32[128]{0:T(128)S(1)} %copy-done.4, s32[128,128]{1,0:T(8,128)S(1)} %add_select_fusion.1), kind=kLoop, calls=%fused_computation.5 | loop fusion | flops 6275072 | bytes 131584 | tf_op jit(solution)/shard_map/reduce_sum | solution.py:76
  17.1 0.0 copy-start.1
  17.1 10.5 %fusion.1 = f32[128,4096,7]{1,0,2:T(8,128)} fusion(bf16[4096,8,128]{0,2,1:T(8,128)(2,1)} %bitcast.69, f32[128,128]{1,0:T(8,128)S(1)} %select_reduce_fusion), kind=kOutput, calls=%fused_computation.7 | convolution fusion | flops 939556864 | bytes 22085632 | tf_op jit(solution)/shard_map/rna,ab->rnb/dot_general | solution.py:86
  27.6 0.0 copy-done.1
  27.6 8.1 %fusion.29 = f32[128,4096,8]{1,0,2:T(8,128)} fusion(bf16[4096,8,128]{0,2,1:T(8,128)(2,1)S(1)} %bitcast.71, f32[128,128]{1,0:T(8,128)S(1)} %select_reduce_fusion), kind=kOutput, calls=%fused_computation.55 | convolution fusion | flops 1073774592 | bytes 25231360 | tf_op jit(solution)/shard_map/rna,ab->rnb/dot_general | solution.py:91
  35.7 0.0 copy-start.2
  35.7 9.4 %add_bitcast_fusion = f32[4096,7,128]{0,2,1:T(8,128)} fusion(f32[128,4096,7]{1,0,2:T(8,128)} %fusion.1, bf16[4096,8,128]{0,2,1:T(8,128)(2,1)S(1)} %bitcast.72, f32[128,128]{1,0:T(8,128)S(1)} %select_reduce_fusion), kind=kOutput, calls=%fused_computation.3 | convolution fusion | flops 943292416 | bytes 36765696 | tf_op jit(solution)/shard_map/rna,ab->rnb/dot_general | solution.py:87
  45.2 0.0 copy-done.2
  45.2 0.7 fusion.48
  47.8 0.6 fusion.20
  48.4 0.2 copy.88
  48.6 0.2 mul.84
  48.8 20.5 %bitcast_add_fusion = f32[4096,8,128]{0,2,1:T(8,128)} fusion(f32[4096,7,128]{0,2,1:T(8,128)} %add_bitcast_fusion, f32[128,4096,8]{1,0,2:T(8,128)} %fusion.29, bf16[4096,8,128]{0,2,1:T(8,128)(2,1)} %bitcast.70, f32[128,128]{1,0:T(8,128)S(1)} %select_reduce_fusion), kind=kOutput, calls=%fused_computation.1 | convolution fusion | flops 1082228736 | bytes 56688640 | tf_op jit(solution)/shard_map/rna,ab->rnb/dot_general | solution.py:94
  69.4 0.0 copy-start
  69.4 7.5 %convolution_bitcast_fusion.1 = f32[64,4096]{1,0:T(8,128)S(1)} fusion(f32[8,128,64]{1,0,2:T(8,128)S(1)} %mul.84, f32[4096,8,128]{0,2,1:T(8,128)} %bitcast_add_fusion), kind=kOutput, calls=%fused_computation.14 | convolution fusion | flops 541065216 | bytes 18087936 | tf_op jit(solution)/shard_map/rnb,nbc->cr/dot_general | solution.py:99
  76.9 3.1 %copy-done = f32[4096,8,128]{0,2,1:T(8,128)S(1)} copy-done((f32[4096,8,128]{0,2,1:T(8,128)S(1)}, f32[4096,8,128]{0,2,1:T(8,128)}, u32[]{:S(2)}) %copy-start) | copy-done | bytes 16777240
  79.9 1.6 fusion.4
  81.5 1.6 fusion.7
  83.1 0.3 reshape.151
  83.4 14.7 %all_to_all.36 = bf16[32,2,1,4096]{3,1,2,0:T(2,128)(2,1)S(1)} all-to-all(bf16[32,2,1,4096]{3,1,2,0:T(2,128)(2,1)S(1)} %bitcast.78), channel_id=1, replica_groups=mesh['freq'=8,'blk'=4] {'freq'}, dimensions={0} | all-to-all | bytes 1048576 | tf_op jit(solution)/shard_map/all_to_all | solution.py:55
  98.1 0.0 copy-start.3
  98.1 9.2 %copy.103 = bf16[4,2,8,4096]{2,0,1,3:T(4,128)(2,1)} copy(bf16[4,2,8,4096]{3,1,0,2:T(2,128)(2,1)S(1)} %bitcast.77) | data formatting | bytes 1048576 | tf_op jit(solution)/shard_map/all_to_all | solution.py:55
  107.4 11.3 %reshape.170 = bf16[4,2,32768]{2,1,0:T(2,128)(2,1)} reshape(bf16[4096,2,4,8]{3,2,1,0:T(4,128)(2,1)} %bitcast.75) | data formatting | bytes 1048576
  118.7 4.8 %all-to-all-start.1 = ((bf16[4,2,32768]{2,1,0:T(2,128)(2,1)}), bf16[4,2,32768]{2,1,0:T(2,128)(2,1)S(1)}, u32[]{:S(2)}, u32[]{:S(2)}) async-start(bf16[4,2,32768]{2,1,0:T(2,128)(2,1)} %reshape.170), calls=%async_computation.1 | async-start | bytes 1048576 | tf_op jit(solution)/shard_map/all_to_all | solution.py:56
  123.5 0.0 copy-done.3
  123.6 13.8 %all-to-all-done.1 = bf16[4,2,32768]{2,1,0:T(2,128)(2,1)S(1)} async-done(((bf16[4,2,32768]{2,1,0:T(2,128)(2,1)}), bf16[4,2,32768]{2,1,0:T(2,128)(2,1)S(1)}, u32[]{:S(2)}, u32[]{:S(2)}) %all-to-all-start.1) | async-done | bytes 524320 | tf_op jit(solution)/shard_map/all_to_all | solution.py:56
  137.4 11.0 %reshape.171 = bf16[4096,2,4,8]{3,2,1,0:T(4,128)(2,1)} reshape(bf16[4,2,32768]{2,1,0:T(2,128)(2,1)S(1)} %all-to-all-done.1) | data formatting | bytes 1048576
  148.4 11.7 %copy.105 = bf16[4,2,4,8,1024]{4,0,3,2,1:T(4,128)(2,1)S(1)} copy(bf16[4,2,4,8,1024]{3,0,1,4,2:T(4,128)(2,1)} %bitcast.73) | data formatting | bytes 1048576 | tf_op jit(solution)/shard_map/all_to_all | solution.py:56
  160.1 0.7 slice.23
  160.8 1.2 gather_fusion
  162.0 0.3 copy.106
  162.3 13.3 %all_gather.3 = bf16[4,2,32,256]{3,2,0,1:T(8,128)(2,1)S(1)} all-gather(bf16[4,2,8,256]{3,2,0,1:T(8,128)(2,1)S(1)} %select_bitcast_fusion), channel_id=1, replica_groups=mesh['freq'=8,'blk'=4] {'blk'}, dimensions={2}, use_global_device_ids=true | all-gather | bytes 163840 | tf_op jit(solution)/shard_map/all_gather | solution.py:57
  175.7 10.8 %copy.108 = bf16[4,2,4,8,1024]{4,3,2,1,0:T(8,128)(2,1)S(1)} copy(bf16[4,2,4,8,1024]{3,0,1,4,2:T(4,128)(2,1)} %bitcast.74) | data formatting | bytes 1048576 | tf_op jit(solution)/shard_map/all_to_all | solution.py:56
  186.5 4.7 %broadcast_multiply_fusion = f32[4,2,256,1024]{3,2,1,0:T(8,128)} fusion(bf16[4,64,1024,1]{2,1,3,0:T(8,128)(2,1)S(1)} %bitcast.76, bf16[4,1,64,256]{3,2,1,0:T(8,128)(2,1)S(1)} %get-tuple-element.8, bf16[4,1,64,256]{3,2,1,0:T(8,128)(2,1)S(1)} %get-tuple-element.7), kind=kOutput, calls=%fused_computation.16 | convolution fusion | flops 270663680 | bytes 9175040 | tf_op jit(solution)/shard_map/fojk,fjr->fokr/dot_general | solution.py:43
  (10 shorter events, 0.1 us)
Async XLA Ops:
  0.0 11.9 %copy-start.4 = (f32[128]{0:T(128)S(1)}, f32[128]{0:T(128)}, u32[]{:S(2)}) copy-start(f32[128]{0:T(128)} %param.5) | copy-start | bytes 1540
  17.1 10.5 %copy-start.1 = (bf16[1,4096,1024]{1,2,0:T(8,128)(2,1)S(1)}, bf16[1,4096,1024]{1,2,0:T(8,128)(2,1)}, u32[]{:S(2)}) copy-start(bf16[1,4096,1024]{1,2,0:T(8,128)(2,1)} %copy.90) | copy-start | bytes 25165828
  35.7 9.5 %copy-start.2 = (s32[2]{0:T(128)S(1)}, s32[2]{0:T(128)}, u32[]{:S(2)}) copy-start(s32[2]{0:T(128)} %param.7) | copy-start | bytes 28
  69.4 10.5 %copy-start = (f32[4096,8,128]{0,2,1:T(8,128)S(1)}, f32[4096,8,128]{0,2,1:T(8,128)}, u32[]{:S(2)}) copy-start(f32[4096,8,128]{0,2,1:T(8,128)} %bitcast_add_fusion) | copy-start | bytes 50331652
  98.1 25.4 %copy-start.3 = (s32[256]{0:T(256)S(1)}, s32[256]{0:T(256)}, u32[]{:S(2)}) copy-start(s32[256]{0:T(256)} %param.6) | copy-start | bytes 3076
  118.7 18.7 %all-to-all-start.1 = ((bf16[4,2,32768]{2,1,0:T(2,128)(2,1)}), bf16[4,2,32768]{2,1,0:T(2,128)(2,1)S(1)}, u32[]{:S(2)}, u32[]{:S(2)}) async-start(bf16[4,2,32768]{2,1,0:T(2,128)(2,1)} %reshape.170), calls=%async_computation.1 | async-start | bytes 1048576 | tf_op jit(solution)/shard_map/all_to_all | solution.py:56
where the time goes:
time: 192 us; the launch traced here: 191 us
  local copies, waits for them, and re-layouts  72.7 us (38%)
  matrix products  63.9 us (33%)
  blocking collectives  28.1 us (15%)
  waiting for transfers between devices  13.8 us (7%)
  other arithmetic  5.83 us (3%)
  starting transfers between devices  4.85 us (3%)
  between operations  2.08 us (1%)
    unnamed x13, local copies, waits for them, and re-layouts  37.3 us
    all_to_all x2, local copies, waits for them, and re-layouts, section_plan(): lax.all_to_all(row_layout, 'blk', split_axis=3, concat_axis=2, tiled=True)  22.5 us
    dot_general x1, matrix products, per_device(): jnp.einsum('rna,ab->rnb', signal, lower_low, preferred_element_type=jnp.f...  20.5 us
    all_to_all x1, blocking collectives, section_plan(): lax.all_to_all(spectrum, 'freq', split_axis=0, concat_axis=2, tiled=True)  14.7 us
    all_to_all x1, waiting for transfers between devices, section_plan(): lax.all_to_all(row_layout, 'blk', split_axis=3, concat_axis=2, tiled=True)  13.8 us
    all_gather x1, blocking collectives, section_plan(): lax.all_gather(local_targets(columns, targets, col_stride), 'blk', axis=2...  13.3 us
    dot_general x1, matrix products, per_device(): jnp.einsum('rna,ab->rnb', earlier, upper_high, preferred_element_type=jnp...  10.5 us
    dot_general x1, matrix products, per_device(): jnp.einsum('rna,ab->rnb', earlier, upper_low, preferred_element_type=jnp....  9.45 us
  transfers between devices with their start and end apart: 1, of which 1 were waited for; matrix products, arithmetic and copies ran while one was open for 0% of the time, Pallas kernels for 0%

commit v1 on v0

--- a/solution.py
+++ b/solution.py
@@ -5,6 +5,18 @@
 from jax.sharding import PartitionSpec as P
 
 FREQ_DEV = 4
+
+
+def gather_by_bits(array, axis, dim):
+    ways, here, step = (lax.axis_size(axis), lax.axis_index(axis), array.shape[dim])
+    line, have = (array, 1)
+    while have < ways:
+        line = jnp.concatenate(
+            [line, lax.ppermute(line, axis, [(d, (d - have) % ways) for d in range(ways)])],
+            axis=dim,
+        )
+        have = 2 * have
+    return jnp.roll(line, here * step, axis=dim)
 
 
 def phase_table(band, freq_count, time_count):
@@ -54,7 +66,7 @@
 def section_plan(spectrum, targets, col_stride, weight_scale):
     row_layout = lax.all_to_all(spectrum, "freq", split_axis=0, concat_axis=2, tiled=True)
     columns = lax.all_to_all(row_layout, "blk", split_axis=3, concat_axis=2, tiled=True)
-    chosen = lax.all_gather(local_targets(columns, targets, col_stride), "blk", axis=2, tiled=True)
+    chosen = gather_by_bits(local_targets(columns, targets, col_stride), "blk", 2)
     return column_products(chosen, columns, weight_scale)
 
 

time: 192 us -> 186 us (0.969)
  blocking collectives: 28.1 us -> 14.7 us
  waiting for transfers between devices: 13.8 us -> 19.6 us
    all_gather x1 -> x0, blocking collectives: 13.3 us -> none  [section_plan(): lax.all_gather(local_targets(columns, targets, col_stride), 'blk', axis=2...]
    ppermute x0 -> x2, waiting for transfers between devices: none -> 5.84 us  [gather_by_bits(): lax.ppermute(line, axis, [(d, (d - have) % ways) for d in range(ways)])]
    unnamed x13 -> x17, local copies, waits for them, and re-layouts: 37.3 us -> 37.3 us
  transfers between devices with their start and end apart: 1 -> 3, of which waited for: 1 -> 2; matrix products, arithmetic and copies ran while one was open for 0% -> 6% of each run, Pallas kernels for 0% -> 0%
where the time goes in v1:
time: 186 us; the launch traced here: 185 us
  local copies, waits for them, and re-layouts  72.7 us (39%)
  matrix products  63.9 us (34%)
  waiting for transfers between devices  19.6 us (11%)
  blocking collectives  14.7 us (8%)
  starting transfers between devices  6.46 us (3%)
  other arithmetic  5.85 us (3%)
  between operations  2.3 us (1%)
    unnamed x17, local copies, waits for them, and re-layouts  37.3 us
    all_to_all x2, local copies, waits for them, and re-layouts, section_plan(): lax.all_to_all(row_layout, 'blk', split_axis=3, concat_axis=2, tiled=True)  22.5 us
    dot_general x1, matrix products, per_device(): jnp.einsum('rna,ab->rnb', signal, lower_low, preferred_element_type=jnp.f...  20.5 us
    all_to_all x1, blocking collectives, section_plan(): lax.all_to_all(spectrum, 'freq', split_axis=0, concat_axis=2, tiled=True)  14.7 us
    all_to_all x1, waiting for transfers between devices, section_plan(): lax.all_to_all(row_layout, 'blk', split_axis=3, concat_axis=2, tiled=True)  13.8 us
    dot_general x1, matrix products, per_device(): jnp.einsum('rna,ab->rnb', earlier, upper_high, preferred_element_type=jnp...  10.5 us
    dot_general x1, matrix products, per_device(): jnp.einsum('rna,ab->rnb', earlier, upper_low, preferred_element_type=jnp....  9.39 us
    all_to_all x1, local copies, waits for them, and re-layouts, section_plan(): lax.all_to_all(spectrum, 'freq', split_axis=0, concat_axis=2, tiled=True)  9.24 us
  transfers between devices with their start and end apart: 3, of which 2 were waited for; matrix products, arithmetic and copies ran while one was open for 6% of the time, Pallas kernels for 0%

profile of v1, /device:TPU:0, one launch (start us, length us, event | category | flops | bytes accessed | tf_op | source)
XLA Modules:
  0.0 185.5 jit_solution(14612912469226271875)
XLA Ops:
  0.0 0.0 copy-start.4
  0.0 11.9 %copy.90 = bf16[1,4096,1024]{1,2,0:T(8,128)(2,1)} copy(bf16[1,4096,1024]{2,1,0:T(8,128)(2,1)} %param.4) | data formatting | bytes 16777216 | tf_op args[0]
  12.0 0.0 copy-done.4
  12.0 5.1 %select_reduce_fusion = f32[128,128]{1,0:T(8,128)S(1)} fusion(f32[128]{0:T(128)S(1)} %copy-done.4, s32[128,128]{1,0:T(8,128)S(1)} %add_select_fusion.1), kind=kLoop, calls=%fused_computation.5 | loop fusion | flops 6275072 | bytes 131584 | tf_op jit(solution)/shard_map/reduce_sum | solution.py:88
  17.1 0.0 copy-start.1
  17.1 10.5 %fusion.1 = f32[128,4096,7]{1,0,2:T(8,128)} fusion(bf16[4096,8,128]{0,2,1:T(8,128)(2,1)} %bitcast.69, f32[128,128]{1,0:T(8,128)S(1)} %select_reduce_fusion), kind=kOutput, calls=%fused_computation.7 | convolution fusion | flops 939556864 | bytes 22085632 | tf_op jit(solution)/shard_map/rna,ab->rnb/dot_general | solution.py:98
  27.6 0.0 copy-done.1
  27.6 8.1 %fusion.29 = f32[128,4096,8]{1,0,2:T(8,128)} fusion(bf16[4096,8,128]{0,2,1:T(8,128)(2,1)S(1)} %bitcast.71, f32[128,128]{1,0:T(8,128)S(1)} %select_reduce_fusion), kind=kOutput, calls=%fused_computation.56 | convolution fusion | flops 1073774592 | bytes 25231360 | tf_op jit(solution)/shard_map/rna,ab->rnb/dot_general | solution.py:103
  35.8 0.0 copy-start.2
  35.8 9.4 %add_bitcast_fusion = f32[4096,7,128]{0,2,1:T(8,128)} fusion(f32[128,4096,7]{1,0,2:T(8,128)} %fusion.1, bf16[4096,8,128]{0,2,1:T(8,128)(2,1)S(1)} %bitcast.72, f32[128,128]{1,0:T(8,128)S(1)} %select_reduce_fusion), kind=kOutput, calls=%fused_computation.3 | convolution fusion | flops 943292416 | bytes 36765696 | tf_op jit(solution)/shard_map/rna,ab->rnb/dot_general | solution.py:99
  45.1 0.0 copy-done.2
  45.2 0.7 fusion.48
  47.9 0.6 fusion.20
  48.5 0.2 copy.88
  48.7 0.2 mul.87
  49.0 20.5 %bitcast_add_fusion = f32[4096,8,128]{0,2,1:T(8,128)} fusion(f32[4096,7,128]{0,2,1:T(8,128)} %add_bitcast_fusion, f32[128,4096,8]{1,0,2:T(8,128)} %fusion.29, bf16[4096,8,128]{0,2,1:T(8,128)(2,1)} %bitcast.70, f32[128,128]{1,0:T(8,128)S(1)} %select_reduce_fusion), kind=kOutput, calls=%fused_computation.1 | convolution fusion | flops 1082228736 | bytes 56688640 | tf_op jit(solution)/shard_map/rna,ab->rnb/dot_general | solution.py:106
  69.5 0.0 copy-start
  69.5 7.5 %convolution_bitcast_fusion.1 = f32[64,4096]{1,0:T(8,128)S(1)} fusion(f32[8,128,64]{1,0,2:T(8,128)S(1)} %mul.87, f32[4096,8,128]{0,2,1:T(8,128)} %bitcast_add_fusion), kind=kOutput, calls=%fused_computation.14 | convolution fusion | flops 541065216 | bytes 18087936 | tf_op jit(solution)/shard_map/rnb,nbc->cr/dot_general | solution.py:111
  77.0 3.1 %copy-done = f32[4096,8,128]{0,2,1:T(8,128)S(1)} copy-done((f32[4096,8,128]{0,2,1:T(8,128)S(1)}, f32[4096,8,128]{0,2,1:T(8,128)}, u32[]{:S(2)}) %copy-start) | copy-done | bytes 16777240
  80.0 1.6 fusion.4
  81.6 1.6 fusion.7
  83.2 0.3 reshape.151
  83.5 14.7 %all_to_all.36 = bf16[32,2,1,4096]{3,1,2,0:T(2,128)(2,1)S(1)} all-to-all(bf16[32,2,1,4096]{3,1,2,0:T(2,128)(2,1)S(1)} %bitcast.78), channel_id=1, replica_groups=mesh['freq'=8,'blk'=4] {'freq'}, dimensions={0} | all-to-all | bytes 1048576 | tf_op jit(solution)/shard_map/all_to_all | solution.py:67
  98.2 0.0 copy-start.3
  98.2 9.2 %copy.103 = bf16[4,2,8,4096]{2,0,1,3:T(4,128)(2,1)} copy(bf16[4,2,8,4096]{3,1,0,2:T(2,128)(2,1)S(1)} %bitcast.77) | data formatting | bytes 1048576 | tf_op jit(solution)/shard_map/all_to_all | solution.py:67
  107.5 11.3 %reshape.170 = bf16[4,2,32768]{2,1,0:T(2,128)(2,1)} reshape(bf16[4096,2,4,8]{3,2,1,0:T(4,128)(2,1)} %bitcast.75) | data formatting | bytes 1048576
  118.8 4.9 %all-to-all-start.1 = ((bf16[4,2,32768]{2,1,0:T(2,128)(2,1)}), bf16[4,2,32768]{2,1,0:T(2,128)(2,1)S(1)}, u32[]{:S(2)}, u32[]{:S(2)}) async-start(bf16[4,2,32768]{2,1,0:T(2,128)(2,1)} %reshape.170), calls=%async_computation.1 | async-start | bytes 1048576 | tf_op jit(solution)/shard_map/all_to_all | solution.py:68
  123.7 0.0 copy-done.3
  123.7 13.8 %all-to-all-done.1 = bf16[4,2,32768]{2,1,0:T(2,128)(2,1)S(1)} async-done(((bf16[4,2,32768]{2,1,0:T(2,128)(2,1)}), bf16[4,2,32768]{2,1,0:T(2,128)(2,1)S(1)}, u32[]{:S(2)}, u32[]{:S(2)}) %all-to-all-start.1) | async-done | bytes 524320 | tf_op jit(solution)/shard_map/all_to_all | solution.py:68
  137.5 11.0 %reshape.171 = bf16[4096,2,4,8]{3,2,1,0:T(4,128)(2,1)} reshape(bf16[4,2,32768]{2,1,0:T(2,128)(2,1)S(1)} %all-to-all-done.1) | data formatting | bytes 1048576
  148.5 11.7 %copy.105 = bf16[4,2,4,8,1024]{4,0,3,2,1:T(4,128)(2,1)S(1)} copy(bf16[4,2,4,8,1024]{3,0,1,4,2:T(4,128)(2,1)} %bitcast.73) | data formatting | bytes 1048576 | tf_op jit(solution)/shard_map/all_to_all | solution.py:68
  160.2 0.7 slice.23
  160.9 1.2 gather_fusion
  162.1 0.3 copy.106
  162.5 1.5 collective-permute-start
  164.0 10.7 %copy.108 = bf16[4,2,4,8,1024]{4,3,2,1,0:T(8,128)(2,1)S(1)} copy(bf16[4,2,4,8,1024]{3,0,1,4,2:T(4,128)(2,1)} %bitcast.74) | data formatting | bytes 1048576 | tf_op jit(solution)/shard_map/all_to_all | solution.py:68
  174.7 0.0 collective-permute-done
  174.7 0.1 collective-permute-start.1
  174.8 5.8 %collective-permute-done.1 = bf16[4,2,16,256]{3,2,0,1:T(8,128)(2,1)S(1)} collective-permute-done((bf16[4,2,16,256]{3,2,0,1:T(8,128)(2,1)S(1)}, bf16[4,2,16,256]{3,2,0,1:T(8,128)(2,1)S(1)}, u32[]{:S(2)}, u32[]{:S(2)}) %collective-permute-start.1) | collective-permute-done | bytes 65568 | tf_op jit(solution)/shard_map/ppermute | solution.py:15
  180.8 4.7 %broadcast_multiply_fusion = f32[4,2,256,1024]{3,2,1,0:T(8,128)} fusion(bf16[4,64,1024,1]{2,1,3,0:T(8,128)(2,1)S(1)} %bitcast.76, bf16[4,1,64,256]{3,2,1,0:T(8,128)(2,1)S(1)} %get-tuple-element.10, bf16[4,1,64,256]{3,2,1,0:T(8,128)(2,1)S(1)} %get-tuple-element.9), kind=kOutput, calls=%fused_computation.16 | convolution fusion | flops 270663680 | bytes 9175040 | tf_op jit(solution)/shard_map/fojk,fjr->fokr/dot_general | solution.py:55
  (16 shorter events, 0.2 us)
Async XLA Ops:
  0.0 11.9 %copy-start.4 = (f32[128]{0:T(128)S(1)}, f32[128]{0:T(128)}, u32[]{:S(2)}) copy-start(f32[128]{0:T(128)} %param.5) | copy-start | bytes 1540
  17.1 10.5 %copy-start.1 = (bf16[1,4096,1024]{1,2,0:T(8,128)(2,1)S(1)}, bf16[1,4096,1024]{1,2,0:T(8,128)(2,1)}, u32[]{:S(2)}) copy-start(bf16[1,4096,1024]{1,2,0:T(8,128)(2,1)} %copy.90) | copy-start | bytes 25165828
  35.8 9.4 %copy-start.2 = (s32[2]{0:T(128)S(1)}, s32[2]{0:T(128)}, u32[]{:S(2)}) copy-start(s32[2]{0:T(128)} %param.7) | copy-start | bytes 28
  69.5 10.5 %copy-start = (f32[4096,8,128]{0,2,1:T(8,128)S(1)}, f32[4096,8,128]{0,2,1:T(8,128)}, u32[]{:S(2)}) copy-start(f32[4096,8,128]{0,2,1:T(8,128)} %bitcast_add_fusion) | copy-start | bytes 50331652
  98.2 25.4 %copy-start.3 = (s32[256]{0:T(256)S(1)}, s32[256]{0:T(256)}, u32[]{:S(2)}) copy-start(s32[256]{0:T(256)} %param.6) | copy-start | bytes 3076
  118.8 18.7 %all-to-all-start.1 = ((bf16[4,2,32768]{2,1,0:T(2,128)(2,1)}), bf16[4,2,32768]{2,1,0:T(2,128)(2,1)S(1)}, u32[]{:S(2)}, u32[]{:S(2)}) async-start(bf16[4,2,32768]{2,1,0:T(2,128)(2,1)} %reshape.170), calls=%async_computation.1 | async-start | bytes 1048576 | tf_op jit(solution)/shard_map/all_to_all | solution.py:68
  162.5 12.3 %collective-permute-start = (bf16[4,2,8,256]{3,2,0,1:T(8,128)(2,1)S(1)}, bf16[4,2,8,256]{3,2,0,1:T(8,128)(2,1)S(1)}, u32[]{:S(2)}, u32[]{:S(2)}) collective-permute-start(bf16[4,2,8,256]{3,2,0,1:T(8,128)(2,1)S(1)} %get-tuple-element.8), channel_id=1, source_target_pairs={{0,3},{1,0},{2,1},{3,2},{4,7},{5,4},{6,5},{7,6},{8,11},{9,8},{10,9... | collective-permute-start | bytes 98312 | tf_op jit(solution)/shard_map/ppermute | solution.py:15
  174.7 5.9 %collective-permute-start.1 = (bf16[4,2,16,256]{3,2,0,1:T(8,128)(2,1)S(1)}, bf16[4,2,16,256]{3,2,0,1:T(8,128)(2,1)S(1)}, u32[]{:S(2)}, u32[]{:S(2)}) collective-permute-start(bf16[4,2,16,256]{3,2,0,1:T(8,128)(2,1)S(1)} %pad_maximum_fusion), channel_id=1, source_target_pairs={{0,2},{1,3},{2,0},{3,1},{4,6},{5,7},{6,4},{7,5},{8,10},{9,11},{10,... | collective-permute-start | bytes 196616 | tf_op jit(solution)/shard_map/ppermute | solution.py:15
